TPU v7x, 32 devices: a whole 2x2x4 slice. The times are simulated.
32 devices in a mesh: dp: 2 (over core), tensor: 16 (over z, y, x).
Axes of the slice: x: 2, y: 2, z: 4, core: 2. Of those that a mesh axis runs over, the one named last changes fastest.
Arguments:
- hidden: bfloat16 [512, 4096], P(('dp', 'tensor')), parts along dimension 0
- norm_gain: float32 [4096], replicated, may hold values from 0.3 to 3
- head_weight: bfloat16 [64128, 4096], P(('dp', 'tensor')), parts along dimension 0
- targets: int32 [512], P(('dp', 'tensor')), parts along dimension 0, may hold values from 0 to 32063
- lengths: int32 [24], P('dp'), parts along dimension 0, may hold values from 1 to 64, as said below
- offsets: int32 [24], P('dp'), parts along dimension 0, may hold values from 0 to 255, as said below
- loss_mask: int32 [512], P(('dp', 'tensor')), parts along dimension 0, may hold values from 0 to 1, as said below
Outputs:
- token_logprob: float32 [512], P(('dp', 'tensor')), parts along dimension 0
- token_entropy: float32 [512], P(('dp', 'tensor')), parts along dimension 0
- sequence_score: float32 [24], P('dp'), parts along dimension 0
There are 2 independent parts, one for each index of `dp`. A program takes and returns all parts, laid end to end along the dimension named above; an argument that names none is the same for every part. Nothing has to cross between parts.
Inputs may be any that keep to these rules, and one draw needn't show every extreme that they name: `lengths`: responses lie in order and do not intersection within the 256 rows; one has length exactly 64. offsets[k] + lengths[k] <= offsets[k+1], and the last response ends within the pack. `loss_mask`: ones only inside responses; the 16 rows of one index of tensor hold at most 10 ones, exactly 10 on some index.
All inputs are finite; a program needn't handle non-finite values.
Results may differ from a plain program's by a relative error of at most 0.0065.
The roundings to bfloat16 on the way count: a program that leaves them out, or rounds other values in their place, can miss the bound.
Values may be sent and summed in bfloat16 or wider, within the bound.
A program may use at most 128 MiB of HBM per device.

v0:
```python
import jax
import jax.numpy as jnp
from jax import lax
from jax.sharding import PartitionSpec as P

epsilon = 1e-05


def row_stats(gathered, gathered_ids, head_weight, vocab_start):
    peaks, sums, spreads, pickeds = ([], [], [], [])
    for row_begin in range(0, gathered.shape[0], 512):
        row_block = gathered[row_begin : row_begin + 512]
        block_ids = gathered_ids[row_begin : row_begin + 512]
        scores = lax.dot_general(
            head_weight, row_block, (((1,), (1,)), ((), ())), preferred_element_type=jnp.float32
        )
        row_peak = jnp.max(scores, axis=0)
        centred = scores - row_peak[None, :]
        expo = jnp.exp(centred)
        sums.append(jnp.sum(expo, axis=0))
        spreads.append(jnp.sum(expo * centred, axis=0))
        column = vocab_start + lax.broadcasted_iota(jnp.int32, scores.shape, 0)
        pickeds.append(jnp.sum(jnp.where(column == block_ids[None, :], scores, 0.0), axis=0))
        peaks.append(row_peak)
    return (
        jnp.concatenate(peaks),
        jnp.concatenate(sums),
        jnp.concatenate(spreads),
        jnp.concatenate(pickeds),
    )


def rescaled(row_peak, row_sum, row_spread, global_peak):
    shift_by = row_peak - global_peak
    factor = jnp.exp(shift_by)
    return (factor * row_sum, factor * (row_spread + shift_by * row_sum))


def local(hidden, norm_gain, head_weight, targets, lengths, offsets, loss_mask):
    own_rows = hidden.shape[0]
    values = hidden.astype(jnp.float32)
    meansq = jnp.mean(values * values, axis=1, keepdims=True)
    normed = (values * lax.rsqrt(meansq + epsilon) * norm_gain[None, :]).astype(jnp.bfloat16)
    width = normed.shape[0]
    gathered, gathered_ids = (
        lax.all_gather(normed, "tensor", axis=0, tiled=True),
        lax.all_gather(targets, "tensor", axis=0, tiled=True),
    )
    shard_index = lax.axis_index("tensor")
    vocab_start = shard_index * head_weight.shape[0]
    row_peak, row_sum, row_spread, picked = row_stats(
        gathered, gathered_ids, head_weight, vocab_start
    )
    own_start = shard_index * width
    global_peak = lax.pmax(row_peak, "tensor")
    scaled_sum, scaled_spread = rescaled(row_peak, row_sum, row_spread, global_peak)
    summed = lax.psum((scaled_sum, scaled_spread, picked), "tensor")
    sum_exp, spread, target_logit = [
        lax.dynamic_slice_in_dim(item, own_start, width) for item in summed
    ]
    final_peak = lax.dynamic_slice_in_dim(global_peak, own_start, width)
    log_total = jnp.log(sum_exp)
    logprob_rows = target_logit - final_peak - log_total
    entropy_rows = log_total - spread / sum_exp
    mask_float = loss_mask.astype(jnp.float32)
    token_logprob = logprob_rows * mask_float
    token_entropy = entropy_rows * mask_float
    positions = shard_index * own_rows + lax.broadcasted_iota(jnp.int32, (own_rows,), 0)
    inside = (positions[None, :] >= offsets[:, None]) & (
        positions[None, :] < (offsets + lengths)[:, None]
    )
    partial_sums = jnp.sum(jnp.where(inside, token_logprob[None, :], 0.0), axis=1)
    seq_totals = lax.psum(partial_sums, "tensor")
    sequence_score = seq_totals / lengths.astype(jnp.float32)
    return (token_logprob, token_entropy, sequence_score)


def solution(mesh):
    return jax.shard_map(
        local,
        mesh=mesh,
        in_specs=(
            P(("dp", "tensor"), None),
            P(),
            P(("dp", "tensor"), None),
            P(("dp", "tensor")),
            P("dp"),
            P("dp"),
            P(("dp", "tensor")),
        ),
        out_specs=(P(("dp", "tensor")), P(("dp", "tensor")), P("dp")),
        check_vma=False,
    )
```

profile of v0, /device:TPU:0, one launch (start us, length us, event | category | flops | bytes accessed | tf_op | source)
XLA Modules:
  0.0 207.0 jit_solution(7430452501256447954)
XLA Ops:
  7.2 0.0 all-gather.2.cloned.1.call-start
  7.2 1.1 fusion.2
  8.3 1.7 fusion.4
  9.9 0.0 all-gather.2.cloned.1.call-update
  10.0 1.2 dynamic-slice
  11.9 0.7 add.52
  12.5 0.8 dynamic-update-slice
  13.4 16.2 %all-reduce = s32[256]{0:T(256)S(1)} all-reduce(s32[256]{0:T(256)S(1)} %dynamic-update-slice), channel_id=1, replica_groups=mesh['dp'=2,'tensor'=16] {'tensor'}, use_global_device_ids=true, to_apply=%add | all-reduce | flops 256 | bytes 2048
  29.6 44.7 %all-gather.2.cloned.1.call-done = bf16[256,4096]{1,0:T(8,128)(2,1)} async-done(((bf16[16,4096]{1,0:T(8,128)(2,1)}), bf16[256,4096]{1,0:T(8,128)(2,1)}) %all-gather.2.cloned.1.call-update) | async-done | bytes 2097168 | tf_op jit(solution)/shard_map/all_gather | solution.py:46
  74.3 8.8 %fusion.5 = (f32[256]{0:T(256)S(1)}, f32[256,2004]{0,1:T(8,128)S(1)}) fusion(bf16[256,4096]{1,0:T(8,128)(2,1)} %all-gather.2.cloned.1.call-done, bf16[2004,4096]{1,0:T(8,128)(2,1)} %param.9), kind=kOutput, calls=%fused_computation.20 | convolution fusion | flops 4203205376 | bytes 20567040 | tf_op jit(solution)/shard_map/dot_general | solution.py:14
  83.1 0.0 copy-start
  83.1 0.0 copy-start.2
  83.1 0.0 copy-start.3
  83.1 39.4 %pmax.7 = f32[256]{0:T(256)S(1)} all-reduce(f32[256]{0:T(256)S(1)} %get-tuple-element.12), channel_id=1, replica_groups=mesh['dp'=2,'tensor'=16] {'tensor'}, use_global_device_ids=true, to_apply=%region_4.5 | all-reduce | flops 256 | bytes 2048 | tf_op jit(solution)/shard_map/pmax | solution.py:55
  122.5 1.0 fusion
  123.6 36.6 %all-reduce.2 = (f32[256]{0:T(256)S(1)}, f32[256]{0:T(256)S(1)}) all-reduce(f32[256]{0:T(256)S(1)} %get-tuple-element.5, f32[256]{0:T(256)S(1)} %get-tuple-element.11), channel_id=1, replica_groups=mesh['dp'=2,'tensor'=16] {'tensor'}, use_global_device_ids=true, to_apply=%region_2.0 | all-reduce | flops 512 | bytes 4096 | tf_op jit(solution)/shard_map/psum | solution.py:57
  160.2 0.0 copy-done
  160.2 0.1 convert_multiply_fusion.2
  160.2 0.0 copy-done.2
  160.2 0.0 copy-start.1
  160.2 0.2 select_reduce_fusion
  160.4 38.6 %all-reduce.1 = (f32[256]{0:T(256)S(1)}, f32[12]{0:T(128)S(1)}) all-reduce(f32[256]{0:T(256)S(1)} %get-tuple-element.10, f32[12]{0:T(128)S(1)} %select_reduce_fusion), channel_id=1, replica_groups=mesh['dp'=2,'tensor'=16] {'tensor'}, use_global_device_ids=true, to_apply=%region_8.9 | all-reduce | flops 268 | bytes 2144 | tf_op jit(solution)/shard_map/psum | solution.py:57
  199.0 0.0 copy-done.3
  199.0 0.5 convert_divide_fusion
  199.6 0.6 subtract_multiply_fusion
  200.2 0.0 copy-done.1
  (5 shorter events, 0.0 us)
Async XLA Ops:
  7.2 67.1 %all-gather.2.cloned.1.call-start = ((), (), s32[]{:S(2)}) async-start(), calls=%async_computation | async-start | bytes 2228224 | tf_op jit(solution)/shard_map/all_gather | solution.py:46
  83.1 77.1 %copy-start = (s32[16]{0:T(128)S(1)}, s32[16]{0:T(128)}, u32[]{:S(2)}) copy-start(s32[16]{0:T(128)} %param.13) | copy-start | bytes 196
  83.1 77.2 %copy-start.2 = (s32[12]{0:T(128)S(1)}, s32[12]{0:T(128)}, u32[]{:S(2)}) copy-start(s32[12]{0:T(128)} %param.12) | copy-start | bytes 148
  83.1 116.0 %copy-start.3 = (s32[12]{0:T(128)S(1)}, s32[12]{0:T(128)}, u32[]{:S(2)}) copy-start(s32[12]{0:T(128)} %param.11) | copy-start | bytes 148
  160.2 39.9 %copy-start.1 = (f32[16]{0:T(128)}, f32[16]{0:T(128)S(1)}, u32[]{:S(2)}) copy-start(f32[16]{0:T(128)S(1)} %convert_multiply_fusion.2) | copy-start | bytes 196
Sparse Core Ops, SparseCore 0:
  10.8 63.4 all-gather.1
where the time goes:
time: 207 us
  blocking collectives  131 us (63%)
  waiting for transfers between devices  44.7 us (22%)
  between operations  14.7 us (7%)
  matrix products  8.78 us (4%)
  other arithmetic  5.84 us (3%)
  local copies, waits for them, and re-layouts  2.11 us (1%)
    psum x2, blocking collectives, local(): summed = lax.psum((scaled_sum, scaled_spread, picked), 'tensor')  75.2 us
    all_gather x1, waiting for transfers between devices, local(): lax.all_gather(normed, 'tensor', axis=0, tiled=True)  44.7 us
    pmax x1, blocking collectives, local(): global_peak = lax.pmax(row_peak, 'tensor')  39.4 us
    unnamed x1, blocking collectives  16.2 us
    dot_general x1, matrix products, row_stats(): lax.dot_general(head_weight, row_block, (((1,), (1,)), ((), ())), preferr...  8.78 us
  transfers between devices with their start and end apart: 1, of which 1 were waited for; matrix products, arithmetic and copies ran while one was open for 1% of the time, Pallas kernels for 0%

commit v1 on v0

v1 whole, which is shorter than its diff:
```python
import functools

import jax
import jax.numpy as jnp
from jax import lax
from jax.experimental import pallas as pl
from jax.experimental.pallas import tpu as pltpu
from jax.sharding import PartitionSpec as P

epsilon = 1e-05
LIVE = 10
MAIN = 8
REST = LIVE - MAIN
TOK = 16
CHUNK = 1024
HALF = CHUNK // 2
PIECE = CHUNK // 8
WIDE = HALF + PIECE
GROUP = 16
MESH = pl.DeviceIdType.MESH


def grid_dims(n):
    for dims in ((4, 2, 2), (4, 4, 4)):
        if dims[0] * dims[1] * dims[2] == n:
            return dims
    return (1, 1, n)


def iota(shape, dim):
    return lax.broadcasted_iota(jnp.int32, shape, dim)


def kernel(
    n,
    targets_ref,
    lengths_ref,
    offsets_ref,
    mask_ref,
    hidden_ref,
    gain_ref,
    weight_ref,
    logprob_ref,
    entropy_ref,
    score_ref,
    head,
    blocks,
    perms,
    rows,
    scores,
    meta,
    stats,
    head_sem,
    send_sem,
    recv_sem,
    meta_send,
    meta_recv,
    stat_send,
    stat_recv,
):
    vocab = weight_ref.shape[0]
    own_rows, width = hidden_ref.shape
    seqs = lengths_ref.shape[0]
    chunks = width // CHUNK
    cols = rows.shape[0]
    na, nb, nc = grid_dims(n)
    me = lax.axis_index("tensor")
    a = me // (nb * nc)
    b = (me // nc) % nb
    c = me % nc

    def at(i, j, k):
        return ((a + i) % na) * (nb * nc) + ((b + j) % nb) * nc + (c + k) % nc

    def head_copy(ch):
        return pltpu.make_async_copy(
            weight_ref.at[:, pl.ds(ch * CHUNK, CHUNK)], head.at[ch], head_sem.at[ch]
        )

    barrier = pltpu.get_barrier_semaphore()

    @pl.loop(1, n)
    def _(p):
        pl.semaphore_signal(
            barrier, inc=1, device_id={"tensor": (me + p) % n}, device_id_type=MESH
        )

    for ch in range(chunks):
        head_copy(ch).start()

    values = hidden_ref[...].astype(jnp.float32)
    meansq = jnp.mean(values * values, axis=1, keepdims=True)
    normed = (values * lax.rsqrt(meansq + epsilon) * gain_ref[...][None, :]).astype(jnp.bfloat16)

    sub = iota((TOK, own_rows), 0)
    lane = iota((TOK, own_rows), 1)
    column = iota((1, cols), 1)
    in_main = column < n * MAIN
    owner = jnp.where(in_main, column // MAIN, (column - n * MAIN) // REST)
    rank_at = jnp.where(in_main, column % MAIN, MAIN + (column - n * MAIN) % REST)
    rank_at = jnp.where(owner == me, rank_at, -1)
    rank_of = jnp.full((TOK, own_rows), -1, jnp.int32)
    ids = jnp.zeros((1, cols), jnp.int32)
    places = jnp.zeros((1, cols), jnp.int32)
    count = jnp.int32(0)
    for i in range(own_rows):
        live = mask_ref[i]
        rank = jnp.where(live == 1, count, -2)
        count = count + live
        rank_of = jnp.where(lane == i, rank, rank_of)
        ids = jnp.where(rank_at == rank, targets_ref[i], ids)
        places = jnp.where(rank_at == rank, me * own_rows + (i + 1), places)
    meta[me, 0:1, :] = ids
    meta[me, 1:2, :] = places

    def choice(begin, first, amount):
        hit = (sub >= begin) & (sub < begin + amount) & (rank_of == sub - begin + first)
        return jnp.where(hit, 1.0, 0.0).astype(jnp.bfloat16)

    def dot(x, y):
        return jnp.dot(x, y, preferred_element_type=jnp.float32)

    halves = [choice(h * MAIN, 0, MAIN) for h in range(2)]
    pieces = [choice(e * REST, MAIN, REST) for e in range(8)]
    for ch in range(chunks):
        base = ch * CHUNK
        packed = sum(
            dot(halves[h], normed[:, base + h * HALF : base + (h + 1) * HALF]) for h in range(2)
        )
        blocks[ch, me, :, 0:HALF] = packed.astype(jnp.bfloat16)
        packed = sum(
            dot(pieces[e], normed[:, base + e * PIECE : base + (e + 1) * PIECE]) for e in range(8)
        )
        blocks[ch, me, :, HALF:WIDE] = packed.astype(jnp.bfloat16)

    pl.semaphore_wait(barrier, n - 1)

    slots = [0] * chunks

    def remote(ch, src, slot, peer):
        return pltpu.make_async_remote_copy(
            src_ref=blocks.at[ch, src],
            dst_ref=blocks.at[ch, src],
            send_sem=send_sem.at[ch, slot],
            recv_sem=recv_sem.at[ch, src],
            device_id={"tensor": peer},
            device_id_type=MESH,
        )

    def send(ch, src, peer):
        remote(ch, src, slots[ch], peer).start()
        slots[ch] += 1

    def arrive(ch, src):
        remote(ch, src, 0, (me + 1) % n).wait_recv()

    def to_b(ch, src):
        for j in range(1, nb):
            send(ch, src, at(0, j, 0))

    def to_c(ch, src):
        for k in range(1, nc):
            send(ch, src, at(0, 0, k))

    def along_a(ch):
        for i in range(1, na):
            send(ch, me, at(i, 0, 0))

    def own(ch):
        to_b(ch, me)
        to_c(ch, me)

    def column_on(ch):
        for i in range(1, na):
            src = at(i, 0, 0)
            arrive(ch, src)
            to_b(ch, src)
            to_c(ch, src)

    early = (na + 1) // 2

    def across(ch):
        for i in range(na):
            if i < early:
                for j in range(1, nb):
                    arrive(ch, at(i, j, 0))
                    to_c(ch, at(i, j, 0))
            else:
                for k in range(1, nc):
                    arrive(ch, at(i, 0, k))
                    to_b(ch, at(i, 0, k))

    def settle(ch):
        for i in range(na):
            if i < early:
                for k in range(1, nc):
                    arrive(ch, at(i, 0, k))
            else:
                for j in range(1, nb):
                    arrive(ch, at(i, j, 0))
            for j in range(1, nb):
                for k in range(1, nc):
                    arrive(ch, at(i, j, k))

    def meta_copy(p):
        return pltpu.make_async_remote_copy(
            src_ref=meta.at[me],
            dst_ref=meta.at[me],
            send_sem=meta_send.at[p],
            recv_sem=meta_recv.at[me],
            device_id={"tensor": (me + p) % n},
            device_id_type=MESH,
        )

    def stat_copy(p):
        return pltpu.make_async_remote_copy(
            src_ref=stats.at[me],
            dst_ref=stats.at[me],
            send_sem=stat_send.at[p],
            recv_sem=stat_recv.at[me],
            device_id={"tensor": (me + p) % n},
            device_id_type=MESH,
        )

    along_a(0)
    own(0)
    for ch in range(1, chunks):
        along_a(ch)
        if ch == 1:
            own(1)

    @pl.loop(1, n)
    def _(p):
        meta_copy(p).start()

    size = GROUP * TOK
    out_row = iota((size, size), 0)
    in_row = iota((size, size), 1)
    span = GROUP * MAIN
    source = (out_row % span) // MAIN * TOK + out_row // span * MAIN + out_row % MAIN
    perms[0] = jnp.where(in_row == source, 1.0, 0.0).astype(jnp.bfloat16)
    span = GROUP * REST
    source = (out_row % span) // REST * TOK + out_row // span * REST + out_row % REST
    perms[1] = jnp.where(in_row == source, 1.0, 0.0).astype(jnp.bfloat16)
    used = n * LIVE
    if used < cols:
        rows[used:cols, :] = jnp.zeros((cols - used, CHUNK), jnp.bfloat16)

    def unpack(ch):
        for g in range(n // GROUP):
            main = blocks[ch, g * GROUP : (g + 1) * GROUP, :, 0:HALF].reshape(size, HALF)
            main = dot(perms[0], main).astype(jnp.bfloat16)
            span = GROUP * MAIN
            for h in range(2):
                rows[g * span : (g + 1) * span, h * HALF : (h + 1) * HALF] = main[
                    h * span : (h + 1) * span
                ]
            rest = blocks[ch, g * GROUP : (g + 1) * GROUP, :, HALF:WIDE].reshape(size, PIECE)
            rest = dot(perms[1], rest).astype(jnp.bfloat16)
            span = GROUP * REST
            top = n * MAIN + g * span
            for e in range(8):
                rows[top : top + span, e * PIECE : (e + 1) * PIECE] = rest[
                    e * span : (e + 1) * span
                ]

    step = 256
    full = vocab // step

    def tiles(body, carry):
        carry = lax.fori_loop(
            0, full, lambda t, v: body(pl.multiple_of(t * step, step), step, v), carry
        )
        if vocab % step:
            carry = body(full * step, vocab % step, carry)
        return carry

    def partial(ch):
        head_copy(ch).wait()

        def body(begin, amount, peak):
            tile = lax.dot_general(
                head[ch, pl.ds(begin, amount), :],
                rows[...],
                (((1,), (1,)), ((), ())),
                preferred_element_type=jnp.float32,
            )
            if ch > 0:
                tile = tile + scores[pl.ds(begin, amount), :]
            scores[pl.ds(begin, amount), :] = tile
            if ch == chunks - 1:
                peak = jnp.maximum(peak, jnp.max(tile, axis=0, keepdims=True))
            return peak

        return tiles(body, jnp.full((1, cols), -jnp.inf, jnp.float32))

    column_on(0)
    if chunks > 1:
        column_on(1)
    across(0)
    if chunks > 2:
        own(2)
    for ch in range(chunks):
        if ch + 2 < chunks:
            column_on(ch + 2)
        if ch + 1 < chunks:
            across(ch + 1)
        if ch + 3 < chunks:
            own(ch + 3)
        settle(ch)
        unpack(ch)
        peak = partial(ch)

    @pl.loop(1, n)
    def _(p):
        other = (me + p) % n
        pltpu.make_async_remote_copy(
            src_ref=meta.at[other],
            dst_ref=meta.at[other],
            send_sem=meta_send.at[p],
            recv_sem=meta_recv.at[other],
            device_id={"tensor": other},
            device_id_type=MESH,
        ).wait_recv()

    ids = sum(meta[s, 0:1, :] for s in range(n))
    places = sum(meta[s, 1:2, :] for s in range(n)) - 1
    local_ids = ids - me * vocab

    def collect(begin, amount, carry):
        row_sum, spread, picked = carry
        tile = scores[pl.ds(begin, amount), :]
        centred = tile - peak
        expo = jnp.exp(centred)
        entry = begin + iota(tile.shape, 0)
        row_sum = row_sum + jnp.sum(expo, axis=0, keepdims=True)
        spread = spread + jnp.sum(expo * centred, axis=0, keepdims=True)
        picked = picked + jnp.sum(
            jnp.where(entry == local_ids, tile, 0.0), axis=0, keepdims=True
        )
        return row_sum, spread, picked

    nothing = jnp.zeros((1, cols), jnp.float32)
    row_sum, spread, picked = tiles(collect, (nothing, nothing, nothing))
    stats[me, 0:1, :] = peak
    stats[me, 1:2, :] = row_sum
    stats[me, 2:3, :] = spread
    stats[me, 3:4, :] = picked

    @pl.loop(1, n)
    def _(p):
        stat_copy(p).start()

    tall = iota((own_rows, cols), 0)
    mine = places == me * own_rows + tall
    kept = iota((seqs, 1), 0)
    first = jnp.zeros((seqs, 1), jnp.int32)
    length = jnp.ones((seqs, 1), jnp.int32)
    for k in range(seqs):
        first = jnp.where(kept == k, offsets_ref[k], first)
        length = jnp.where(kept == k, lengths_ref[k], length)
    inside = (places >= first) & (places < first + length)

    @pl.loop(1, n)
    def _(p):
        other = (me + p) % n
        pltpu.make_async_remote_copy(
            src_ref=stats.at[other],
            dst_ref=stats.at[other],
            send_sem=stat_send.at[p],
            recv_sem=stat_recv.at[other],
            device_id={"tensor": other},
            device_id_type=MESH,
        ).wait_recv()

    top = functools.reduce(jnp.maximum, [stats[s, 0:1, :] for s in range(n)])
    sum_exp, spread, picked = nothing, nothing, nothing
    for s in range(n):
        shift = stats[s, 0:1, :] - top
        factor = jnp.exp(shift)
        part = stats[s, 1:2, :]
        sum_exp = sum_exp + factor * part
        spread = spread + factor * (stats[s, 2:3, :] + shift * part)
        picked = picked + stats[s, 3:4, :]
    log_total = jnp.log(sum_exp)
    logprob = picked - top - log_total
    entropy = log_total - spread / sum_exp

    def lay(col):
        amount = col.shape[0]
        square = iota((amount, amount), 0) == iota((amount, amount), 1)
        return jnp.sum(jnp.where(square, col, 0.0), axis=0, keepdims=True)

    def total(where, value):
        return jnp.sum(jnp.where(where, value, 0.0), axis=1, keepdims=True)

    logprob_ref[...] = lay(total(mine, logprob))
    entropy_ref[...] = lay(total(mine, entropy))
    score_ref[...] = lay(total(inside, logprob) / length.astype(jnp.float32))

    for ch in range(chunks):
        for slot in range(slots[ch]):
            remote(ch, me, slot, (me + 1) % n).wait_send()

    @pl.loop(1, n)
    def _(p):
        meta_copy(p).wait_send()
        stat_copy(p).wait_send()


def local(n, hidden, norm_gain, head_weight, targets, lengths, offsets, loss_mask):
    own_rows, width = hidden.shape
    vocab = head_weight.shape[0]
    seqs = lengths.shape[0]
    chunks = width // CHUNK
    cols = -(-n * LIVE // 128) * 128
    smem = pl.BlockSpec(memory_space=pltpu.SMEM)
    vmem = pl.BlockSpec(memory_space=pltpu.VMEM)
    dma = pltpu.SemaphoreType.DMA
    logprob, entropy, score = pl.pallas_call(
        functools.partial(kernel, n),
        out_shape=(
            jax.ShapeDtypeStruct((1, own_rows), jnp.float32),
            jax.ShapeDtypeStruct((1, own_rows), jnp.float32),
            jax.ShapeDtypeStruct((1, seqs), jnp.float32),
        ),
        in_specs=[smem] * 4 + [vmem, vmem, pl.BlockSpec(memory_space=pl.ANY)],
        out_specs=(vmem, vmem, vmem),
        scratch_shapes=[
            pltpu.VMEM((chunks, vocab, CHUNK), jnp.bfloat16),
            pltpu.VMEM((chunks, n, TOK, WIDE), jnp.bfloat16),
            pltpu.VMEM((2, GROUP * TOK, GROUP * TOK), jnp.bfloat16),
            pltpu.VMEM((cols, CHUNK), jnp.bfloat16),
            pltpu.VMEM((vocab, cols), jnp.float32),
            pltpu.VMEM((n, 2, cols), jnp.int32),
            pltpu.VMEM((n, 4, cols), jnp.float32),
            dma((chunks,)),
            dma((chunks, n)),
            dma((chunks, n)),
            dma((n,)),
            dma((n,)),
            dma((n,)),
            dma((n,)),
        ],
        compiler_params=pltpu.CompilerParams(
            collective_id=0, has_side_effects=True, vmem_limit_bytes=48 * 2**20
        ),
        cost_estimate=pl.CostEstimate(
            flops=2 * vocab * width * n * LIVE,
            bytes_accessed=2 * vocab * width,
            transcendentals=vocab * n * LIVE,
        ),
        name="head_stats",
    )(targets, lengths, offsets, loss_mask, hidden, norm_gain, head_weight)
    return logprob.reshape(own_rows), entropy.reshape(own_rows), score.reshape(seqs)


def solution(mesh):
    return jax.shard_map(
        functools.partial(local, mesh.shape["tensor"]),
        mesh=mesh,
        in_specs=(
            P(("dp", "tensor"), None),
            P(),
            P(("dp", "tensor"), None),
            P(("dp", "tensor")),
            P("dp"),
            P("dp"),
            P(("dp", "tensor")),
        ),
        out_specs=(P(("dp", "tensor")), P(("dp", "tensor")), P("dp")),
        check_vma=False,
    )
```

time: 207 us -> 46.4 us (0.22)
  blocking collectives: 131 us -> 0 us
  waiting for transfers between devices: 44.7 us -> 0 us
  Pallas kernels: 0 us -> 39.7 us
  between operations: 14.7 us -> 0.66 us
  matrix products: 8.78 us -> 0 us
  other arithmetic: 5.84 us -> 0 us
  local copies, waits for them, and re-layouts: 2.11 us -> 5.77 us
    psum x2 -> x0, blocking collectives: 75.2 us -> none  [local(): summed = lax.psum((scaled_sum, scaled_spread, picked), 'tensor')]
    all_gather x1 -> x0, waiting for transfers between devices: 44.7 us -> none  [local(): lax.all_gather(normed, 'tensor', axis=0, tiled=True)]
    pallas_call x0 -> x1, Pallas kernels: none -> 39.7 us  [local(): pl.pallas_call(functools.partial(kernel, n), out_shape=(jax.ShapeDtypeStr...]
    pmax x1 -> x0, blocking collectives: 39.4 us -> none  [local(): global_peak = lax.pmax(row_peak, 'tensor')]
    unnamed x1 -> x0, blocking collectives: 16.2 us -> none
    dot_general x1 -> x0, matrix products: 8.78 us -> none  [row_stats(): lax.dot_general(head_weight, row_block, (((1,), (1,)), ((), ())), preferr...]
    unnamed x11 -> x15, local copies, waits for them, and re-layouts: 2.11 us -> 5.77 us
    reduce_sum x3 -> x0, other arithmetic: 2.28 us -> none  [the longest x1 1.05 us: local(): meansq = jnp.mean(values * values, axis=1, keepdims=True)]
  transfers between devices with their start and end apart: 1 -> 0, of which waited for: 1 -> 0; matrix products, arithmetic and copies ran while one was open for 1% -> 0% of each run, Pallas kernels for 0% -> 0%
where the time goes in v1:
time: 46.4 us; the launch traced here: 46.2 us
  Pallas kernels  39.7 us (86%)
  local copies, waits for them, and re-layouts  5.77 us (12%)
  between operations  0.66 us (1%)
    pallas_call x1, Pallas kernels, local(): pl.pallas_call(functools.partial(kernel, n), out_shape=(jax.ShapeDtypeStr...  39.7 us
    unnamed x15, local copies, waits for them, and re-layouts  5.77 us

profile of v1, /device:TPU:0, one launch (start us, length us, event | category | flops | bytes accessed | tf_op | source)
XLA Modules:
  0.0 46.2 jit_solution(4460251821364040658)
XLA Ops:
  0.6 0.0 copy-start
  0.6 0.9 %copy-done = bf16[16,4096]{1,0:T(8,128)(2,1)S(1)} copy-done((bf16[16,4096]{1,0:T(8,128)(2,1)S(1)}, bf16[16,4096]{1,0:T(8,128)(2,1)}, u32[]{:S(2)}) %copy-start) | copy-done | bytes 131096
  1.5 0.0 copy-start.1
  1.5 0.7 %copy-done.1 = f32[4096]{0:T(1024)S(1)} copy-done((f32[4096]{0:T(1024)S(1)}, f32[4096]{0:T(1024)}, u32[]{:S(2)}) %copy-start.1) | copy-done | bytes 16408
  2.3 0.0 copy-start.2
  2.3 0.7 %copy-done.2 = s32[16]{0:T(128)S(1)} copy-done((s32[16]{0:T(128)S(1)}, s32[16]{0:T(128)}, u32[]{:S(2)}) %copy-start.2) | copy-done | bytes 88
  2.9 0.0 copy-start.3
  2.9 0.7 %copy-done.3 = s32[12]{0:T(128)S(1)} copy-done((s32[12]{0:T(128)S(1)}, s32[12]{0:T(128)}, u32[]{:S(2)}) %copy-start.3) | copy-done | bytes 72
  3.6 0.0 copy-start.4
  3.6 0.7 %copy-done.4 = s32[12]{0:T(128)S(1)} copy-done((s32[12]{0:T(128)S(1)}, s32[12]{0:T(128)}, u32[]{:S(2)}) %copy-start.4) | copy-done | bytes 72
  4.2 0.0 copy-start.5
  4.2 0.7 %copy-done.5 = s32[16]{0:T(128)S(1)} copy-done((s32[16]{0:T(128)S(1)}, s32[16]{0:T(128)}, u32[]{:S(2)}) %copy-start.5) | copy-done | bytes 88
  4.9 39.7 %head_stats.1 = (f32[1,16]{1,0:T(1,128)S(1)}, f32[1,16]{1,0:T(1,128)S(1)}, f32[1,12]{1,0:T(1,128)S(1)}) custom-call(s32[16]{0:T(128)S(1)} %copy-done.2, s32[12]{0:T(128)S(1)} %copy-done.3, s32[12]{0:T(128)S(1)} %copy-done.4, s32[16]{0:T(128)S(1)} %copy-done.5, bf16[16,4096]{1,0:T(8,128)(2,1)S(1)} %copy-done, f32[4096]{0:T(1024)S(1)} %copy-done.1, ...), custom_call_target="tpu_custom_call" | custom-call | flops 2626682880 | bytes 16416768 | tf_op jit(solution)/shard_map/head_stats/pallas_call | solution.py:420
  44.6 0.5 %copy.13 = f32[16]{0:T(128)} copy(f32[16]{0:T(128)S(1)} %bitcast.5) | data formatting | bytes 128
  45.1 0.5 %copy.14 = f32[16]{0:T(128)} copy(f32[16]{0:T(128)S(1)} %bitcast.4) | data formatting | bytes 128
  45.6 0.5 %copy.15 = f32[12]{0:T(128)} copy(f32[12]{0:T(128)S(1)} %bitcast.3) | data formatting | bytes 96
Async XLA Ops:
  0.6 0.9 %copy-start = (bf16[16,4096]{1,0:T(8,128)(2,1)S(1)}, bf16[16,4096]{1,0:T(8,128)(2,1)}, u32[]{:S(2)}) copy-start(bf16[16,4096]{1,0:T(8,128)(2,1)} %hidden_ref.1) | copy-start | bytes 393220
  1.5 0.7 %copy-start.1 = (f32[4096]{0:T(1024)S(1)}, f32[4096]{0:T(1024)}, u32[]{:S(2)}) copy-start(f32[4096]{0:T(1024)} %gain_ref.1) | copy-start | bytes 49156
  2.3 0.7 %copy-start.2 = (s32[16]{0:T(128)S(1)}, s32[16]{0:T(128)}, u32[]{:S(2)}) copy-start(s32[16]{0:T(128)} %targets_ref.1) | copy-start | bytes 196
  2.9 0.7 %copy-start.3 = (s32[12]{0:T(128)S(1)}, s32[12]{0:T(128)}, u32[]{:S(2)}) copy-start(s32[12]{0:T(128)} %lengths_ref.1) | copy-start | bytes 148
  3.6 0.7 %copy-start.4 = (s32[12]{0:T(128)S(1)}, s32[12]{0:T(128)}, u32[]{:S(2)}) copy-start(s32[12]{0:T(128)} %offsets_ref.1) | copy-start | bytes 148
  4.2 0.7 %copy-start.5 = (s32[16]{0:T(128)S(1)}, s32[16]{0:T(128)}, u32[]{:S(2)}) copy-start(s32[16]{0:T(128)} %mask_ref.1) | copy-start | bytes 196

commit v2 on v1

--- a/solution.py
+++ b/solution.py
@@ -33,23 +33,31 @@
 
 def kernel(
     n,
+    targets_hbm,
+    lengths_hbm,
+    offsets_hbm,
+    mask_hbm,
+    hidden_hbm,
+    gain_hbm,
+    weight_ref,
+    logprob_ref,
+    entropy_ref,
+    score_ref,
     targets_ref,
     lengths_ref,
     offsets_ref,
     mask_ref,
     hidden_ref,
     gain_ref,
-    weight_ref,
-    logprob_ref,
-    entropy_ref,
-    score_ref,
     head,
     blocks,
-    perms,
+    main_perm,
+    rest_perm,
     rows,
     scores,
     meta,
     stats,
+    in_sem,
     head_sem,
     send_sem,
     recv_sem,
@@ -62,7 +70,7 @@
     own_rows, width = hidden_ref.shape
     seqs = lengths_ref.shape[0]
     chunks = width // CHUNK
-    cols = rows.shape[0]
+    cols = rows.shape[1]
     na, nb, nc = grid_dims(n)
     me = lax.axis_index("tensor")
     a = me // (nb * nc)
@@ -85,8 +93,25 @@
             barrier, inc=1, device_id={"tensor": (me + p) % n}, device_id_type=MESH
         )
 
+    small = [
+        pltpu.make_async_copy(there, here, in_sem.at[i])
+        for i, (there, here) in enumerate(
+            (
+                (hidden_hbm, hidden_ref),
+                (gain_hbm, gain_ref),
+                (mask_hbm, mask_ref),
+                (targets_hbm, targets_ref),
+                (lengths_hbm, lengths_ref),
+                (offsets_hbm, offsets_ref),
+            )
+        )
+    ]
+    for copy in small:
+        copy.start()
     for ch in range(chunks):
         head_copy(ch).start()
+    for copy in small:
+        copy.wait()
 
     values = hidden_ref[...].astype(jnp.float32)
     meansq = jnp.mean(values * values, axis=1, keepdims=True)
@@ -94,24 +119,14 @@
 
     sub = iota((TOK, own_rows), 0)
     lane = iota((TOK, own_rows), 1)
-    column = iota((1, cols), 1)
-    in_main = column < n * MAIN
-    owner = jnp.where(in_main, column // MAIN, (column - n * MAIN) // REST)
-    rank_at = jnp.where(in_main, column % MAIN, MAIN + (column - n * MAIN) % REST)
-    rank_at = jnp.where(owner == me, rank_at, -1)
     rank_of = jnp.full((TOK, own_rows), -1, jnp.int32)
-    ids = jnp.zeros((1, cols), jnp.int32)
-    places = jnp.zeros((1, cols), jnp.int32)
+    ranks = []
     count = jnp.int32(0)
     for i in range(own_rows):
         live = mask_ref[i]
-        rank = jnp.where(live == 1, count, -2)
+        ranks.append(jnp.where(live == 1, count, -2))
         count = count + live
-        rank_of = jnp.where(lane == i, rank, rank_of)
-        ids = jnp.where(rank_at == rank, targets_ref[i], ids)
-        places = jnp.where(rank_at == rank, me * own_rows + (i + 1), places)
-    meta[me, 0:1, :] = ids
-    meta[me, 1:2, :] = places
+        rank_of = jnp.where(lane == i, ranks[i], rank_of)
 
     def choice(begin, first, amount):
         hit = (sub >= begin) & (sub < begin + amount) & (rank_of == sub - begin + first)
@@ -122,7 +137,8 @@
 
     halves = [choice(h * MAIN, 0, MAIN) for h in range(2)]
     pieces = [choice(e * REST, MAIN, REST) for e in range(8)]
-    for ch in range(chunks):
+
+    def pack(ch):
         base = ch * CHUNK
         packed = sum(
             dot(halves[h], normed[:, base + h * HALF : base + (h + 1) * HALF]) for h in range(2)
@@ -132,8 +148,6 @@
             dot(pieces[e], normed[:, base + e * PIECE : base + (e + 1) * PIECE]) for e in range(8)
         )
         blocks[ch, me, :, HALF:WIDE] = packed.astype(jnp.bfloat16)
-
-    pl.semaphore_wait(barrier, n - 1)
 
     slots = [0] * chunks
 
@@ -222,69 +236,90 @@
             device_id_type=MESH,
         )
 
+    pack(0)
+    pl.semaphore_wait(barrier, n - 1)
     along_a(0)
     own(0)
     for ch in range(1, chunks):
+        pack(ch)
         along_a(ch)
         if ch == 1:
             own(1)
 
+    column = iota((1, cols), 1)
+    in_main = column < n * MAIN
+    owner = jnp.where(in_main, column // MAIN, (column - n * MAIN) // REST)
+    rank_at = jnp.where(in_main, column % MAIN, MAIN + (column - n * MAIN) % REST)
+    rank_at = jnp.where(owner == me, rank_at, -1)
+    ids = jnp.zeros((1, cols), jnp.int32)
+    places = jnp.zeros((1, cols), jnp.int32)
+    for i in range(own_rows):
+        ids = jnp.where(rank_at == ranks[i], targets_ref[i], ids)
+        places = jnp.where(rank_at == ranks[i], me * own_rows + (i + 1), places)
+    meta[me, 0:1, :] = ids
+    meta[me, 1:2, :] = places
+
     @pl.loop(1, n)
     def _(p):
         meta_copy(p).start()
 
+    groups = n // GROUP
     size = GROUP * TOK
-    out_row = iota((size, size), 0)
-    in_row = iota((size, size), 1)
+    in_row = iota((size, size), 0)
+    out_col = iota((size, size), 1)
     span = GROUP * MAIN
-    source = (out_row % span) // MAIN * TOK + out_row // span * MAIN + out_row % MAIN
-    perms[0] = jnp.where(in_row == source, 1.0, 0.0).astype(jnp.bfloat16)
-    span = GROUP * REST
-    source = (out_row % span) // REST * TOK + out_row // span * REST + out_row % REST
-    perms[1] = jnp.where(in_row == source, 1.0, 0.0).astype(jnp.bfloat16)
-    used = n * LIVE
-    if used < cols:
-        rows[used:cols, :] = jnp.zeros((cols - used, CHUNK), jnp.bfloat16)
+    source = (out_col % span) // MAIN * TOK + out_col // span * MAIN + out_col % MAIN
+    main_perm[...] = jnp.where(in_row == source, 1.0, 0.0).astype(jnp.bfloat16)
+    tail = cols - n * MAIN
+    in_row = iota((size, tail), 0)
+    for g in range(groups):
+        out_col = iota((size, tail), 1) - g * GROUP * REST
+        valid = (out_col >= 0) & (out_col < GROUP * REST)
+        for e in range(8):
+            source = out_col // REST * TOK + e * REST + out_col % REST
+            rest_perm[g * 8 + e] = jnp.where(valid & (in_row == source), 1.0, 0.0).astype(
+                jnp.bfloat16
+            )
+
+    def turned(x, y):
+        return lax.dot_general(
+            x, y, (((0,), (0,)), ((), ())), preferred_element_type=jnp.float32
+        )
 
     def unpack(ch):
-        for g in range(n // GROUP):
-            main = blocks[ch, g * GROUP : (g + 1) * GROUP, :, 0:HALF].reshape(size, HALF)
-            main = dot(perms[0], main).astype(jnp.bfloat16)
-            span = GROUP * MAIN
+        span = GROUP * MAIN
+        tops = [
+            blocks[ch, g * GROUP : (g + 1) * GROUP, :, 0:HALF].reshape(size, HALF)
+            for g in range(groups)
+        ]
+        rests = [
+            blocks[ch, g * GROUP : (g + 1) * GROUP, :, HALF:WIDE].reshape(size, PIECE)
+            for g in range(groups)
+        ]
+        for g in range(groups):
+            main = turned(tops[g], main_perm[...]).astype(jnp.bfloat16)
             for h in range(2):
-                rows[g * span : (g + 1) * span, h * HALF : (h + 1) * HALF] = main[
-                    h * span : (h + 1) * span
+                rows[h * HALF : (h + 1) * HALF, g * span : (g + 1) * span] = main[
+                    :, h * span : (h + 1) * span
                 ]
-            rest = blocks[ch, g * GROUP : (g + 1) * GROUP, :, HALF:WIDE].reshape(size, PIECE)
-            rest = dot(perms[1], rest).astype(jnp.bfloat16)
-            span = GROUP * REST
-            top = n * MAIN + g * span
-            for e in range(8):
-                rows[top : top + span, e * PIECE : (e + 1) * PIECE] = rest[
-                    e * span : (e + 1) * span
-                ]
-
-    step = 256
-    full = vocab // step
-
-    def tiles(body, carry):
+        for e in range(8):
+            rest = sum(turned(rests[g], rest_perm[g * 8 + e]) for g in range(groups))
+            rows[e * PIECE : (e + 1) * PIECE, n * MAIN : cols] = rest.astype(jnp.bfloat16)
+
+    def tiles(extent, step, body, carry):
+        full = extent // step
         carry = lax.fori_loop(
             0, full, lambda t, v: body(pl.multiple_of(t * step, step), step, v), carry
         )
-        if vocab % step:
-            carry = body(full * step, vocab % step, carry)
+        if extent % step:
+            carry = body(full * step, extent % step, carry)
         return carry
 
     def partial(ch):
         head_copy(ch).wait()
 
         def body(begin, amount, peak):
-            tile = lax.dot_general(
-                head[ch, pl.ds(begin, amount), :],
-                rows[...],
-                (((1,), (1,)), ((), ())),
-                preferred_element_type=jnp.float32,
-            )
+            tile = dot(head[ch, pl.ds(begin, amount), :], rows[...])
             if ch > 0:
                 tile = tile + scores[pl.ds(begin, amount), :]
             scores[pl.ds(begin, amount), :] = tile
@@ -292,7 +327,11 @@
                 peak = jnp.maximum(peak, jnp.max(tile, axis=0, keepdims=True))
             return peak
 
-        return tiles(body, jnp.full((1, cols), -jnp.inf, jnp.float32))
+        return tiles(vocab, 512, body, jnp.full((1, cols), -jnp.inf, jnp.float32))
+
+    padded = scores.shape[0]
+    if padded > vocab:
+        scores[vocab:padded, :] = jnp.full((padded - vocab, cols), -1e30, jnp.float32)
 
     column_on(0)
     if chunks > 1:
@@ -326,6 +365,7 @@
     ids = sum(meta[s, 0:1, :] for s in range(n))
     places = sum(meta[s, 1:2, :] for s in range(n)) - 1
     local_ids = ids - me * vocab
+    local_ids = jnp.where(local_ids < vocab, local_ids, -1)
 
     def collect(begin, amount, carry):
         row_sum, spread, picked = carry
@@ -333,15 +373,19 @@
         centred = tile - peak
         expo = jnp.exp(centred)
         entry = begin + iota(tile.shape, 0)
-        row_sum = row_sum + jnp.sum(expo, axis=0, keepdims=True)
-        spread = spread + jnp.sum(expo * centred, axis=0, keepdims=True)
-        picked = picked + jnp.sum(
-            jnp.where(entry == local_ids, tile, 0.0), axis=0, keepdims=True
-        )
-        return row_sum, spread, picked
-
-    nothing = jnp.zeros((1, cols), jnp.float32)
-    row_sum, spread, picked = tiles(collect, (nothing, nothing, nothing))
+        given = jnp.where(entry == local_ids, tile, 0.0)
+
+        def fold(x):
+            return jnp.sum(x.reshape(amount // 8, 8, cols), axis=0)
+
+        return row_sum + fold(expo), spread + fold(expo * centred), picked + fold(given)
+
+    nothing = jnp.zeros((8, cols), jnp.float32)
+    row_sum, spread, picked = (
+        jnp.sum(x, axis=0, keepdims=True)
+        for x in tiles(padded, 64, collect, (nothing, nothing, nothing))
+    )
+    nothing = nothing[0:1]
     stats[me, 0:1, :] = peak
     stats[me, 1:2, :] = row_sum
     stats[me, 2:3, :] = spread
@@ -413,8 +457,8 @@
     vocab = head_weight.shape[0]
     seqs = lengths.shape[0]
     chunks = width // CHUNK
-    cols = -(-n * LIVE // 128) * 128
-    smem = pl.BlockSpec(memory_space=pltpu.SMEM)
+    cols = n * MAIN + 128
+    hbm = pl.BlockSpec(memory_space=pltpu.HBM)
     vmem = pl.BlockSpec(memory_space=pltpu.VMEM)
     dma = pltpu.SemaphoreType.DMA
     logprob, entropy, score = pl.pallas_call(
@@ -424,16 +468,24 @@
             jax.ShapeDtypeStruct((1, own_rows), jnp.float32),
             jax.ShapeDtypeStruct((1, seqs), jnp.float32),
         ),
-        in_specs=[smem] * 4 + [vmem, vmem, pl.BlockSpec(memory_space=pl.ANY)],
+        in_specs=[hbm] * 7,
         out_specs=(vmem, vmem, vmem),
         scratch_shapes=[
+            pltpu.SMEM((own_rows,), jnp.int32),
+            pltpu.SMEM((seqs,), jnp.int32),
+            pltpu.SMEM((seqs,), jnp.int32),
+            pltpu.SMEM((own_rows,), jnp.int32),
+            pltpu.VMEM((own_rows, width), jnp.bfloat16),
+            pltpu.VMEM((width,), jnp.float32),
             pltpu.VMEM((chunks, vocab, CHUNK), jnp.bfloat16),
             pltpu.VMEM((chunks, n, TOK, WIDE), jnp.bfloat16),
-            pltpu.VMEM((2, GROUP * TOK, GROUP * TOK), jnp.bfloat16),
-            pltpu.VMEM((cols, CHUNK), jnp.bfloat16),
-            pltpu.VMEM((vocab, cols), jnp.float32),
+            pltpu.VMEM((GROUP * TOK, GROUP * TOK), jnp.bfloat16),
+            pltpu.VMEM((n // GROUP * 8, GROUP * TOK, 128), jnp.bfloat16),
+            pltpu.VMEM((CHUNK, cols), jnp.bfloat16),
+            pltpu.VMEM((-(-vocab // 8) * 8, cols), jnp.float32),
             pltpu.VMEM((n, 2, cols), jnp.int32),
             pltpu.VMEM((n, 4, cols), jnp.float32),
+            dma((6,)),
             dma((chunks,)),
             dma((chunks, n)),
             dma((chunks, n)),
@@ -443,7 +495,7 @@
             dma((n,)),
         ],
         compiler_params=pltpu.CompilerParams(
-            collective_id=0, has_side_effects=True, vmem_limit_bytes=48 * 2**20
+            collective_id=0, has_side_effects=True, vmem_limit_bytes=64 * 2**20
         ),
         cost_estimate=pl.CostEstimate(
             flops=2 * vocab * width * n * LIVE,

time: 46.4 us -> 41.9 us (0.903)
  local copies, waits for them, and re-layouts: 5.77 us -> 3.42 us
  Pallas kernels: 39.7 us -> 37.6 us
    unnamed x15 -> x3, local copies, waits for them, and re-layouts: 5.77 us -> 3.42 us
    pallas_call x1, Pallas kernels: 39.7 us -> 37.6 us  [local(): pl.pallas_call(functools.partial(kernel, n), out_shape=(jax.ShapeDtypeStr...]
where the time goes in v2:
time: 41.9 us; the launch traced here: 41.7 us
  Pallas kernels  37.6 us (90%)
  local copies, waits for them, and re-layouts  3.42 us (8%)
  between operations  0.64 us (2%)
    pallas_call x1, Pallas kernels, local(): pl.pallas_call(functools.partial(kernel, n), out_shape=(jax.ShapeDtypeStr...  37.6 us
    unnamed x3, local copies, waits for them, and re-layouts  3.42 us

profile of v2, /device:TPU:0, one launch (start us, length us, event | category | flops | bytes accessed | tf_op | source)
XLA Modules:
  0.0 41.7 jit_solution(17096860082598403936)
XLA Ops:
  0.6 37.6 %head_stats.1 = (f32[1,16]{1,0:T(1,128)}, f32[1,16]{1,0:T(1,128)}, f32[1,12]{1,0:T(1,128)}) custom-call(s32[16]{0:T(128)} %targets_hbm.1, s32[12]{0:T(128)} %lengths_hbm.1, s32[12]{0:T(128)} %offsets_hbm.1, s32[16]{0:T(128)} %mask_hbm.1, bf16[16,4096]{1,0:T(8,128)(2,1)} %hidden_hbm.1, f32[4096]{0:T(1024)} %gain_hbm.1, bf16[2004,4096]{1,0:T(8,128)(2,1)} %weight_ref.1), custom_call_target="tpu_custom_call" | custom-call | flops 2626682880 | bytes 16416768 | tf_op jit(solution)/shard_map/head_stats/pallas_call | solution.py:464
  38.3 1.1 %copy.13 = f32[16]{0:T(128)} copy(f32[16]{0:T(128)} %bitcast.5) | data formatting | bytes 128
  39.4 1.1 %copy.14 = f32[16]{0:T(128)} copy(f32[16]{0:T(128)} %bitcast.4) | data formatting | bytes 128
  40.5 1.2 %copy.15 = f32[12]{0:T(128)} copy(f32[12]{0:T(128)} %bitcast.3) | data formatting | bytes 96

commit v3 on v2

--- a/solution.py
+++ b/solution.py
@@ -40,9 +40,7 @@
     hidden_hbm,
     gain_hbm,
     weight_ref,
-    logprob_ref,
-    entropy_ref,
-    score_ref,
+    result_ref,
     targets_ref,
     lengths_ref,
     offsets_ref,
@@ -243,8 +241,7 @@
     for ch in range(1, chunks):
         pack(ch)
         along_a(ch)
-        if ch == 1:
-            own(1)
+        own(ch)
 
     column = iota((1, cols), 1)
     in_main = column < n * MAIN
@@ -262,6 +259,10 @@
     @pl.loop(1, n)
     def _(p):
         meta_copy(p).start()
+
+    column_on(0)
+    if chunks > 1:
+        column_on(1)
 
     groups = n // GROUP
     size = GROUP * TOK
@@ -333,19 +334,16 @@
     if padded > vocab:
         scores[vocab:padded, :] = jnp.full((padded - vocab, cols), -1e30, jnp.float32)
 
-    column_on(0)
-    if chunks > 1:
-        column_on(1)
     across(0)
     if chunks > 2:
-        own(2)
+        column_on(2)
+    if chunks > 1:
+        across(1)
     for ch in range(chunks):
+        if ch + 3 < chunks:
+            column_on(ch + 3)
         if ch + 2 < chunks:
-            column_on(ch + 2)
-        if ch + 1 < chunks:
-            across(ch + 1)
-        if ch + 3 < chunks:
-            own(ch + 3)
+            across(ch + 2)
         settle(ch)
         unpack(ch)
         peak = partial(ch)
@@ -438,9 +436,9 @@
     def total(where, value):
         return jnp.sum(jnp.where(where, value, 0.0), axis=1, keepdims=True)
 
-    logprob_ref[...] = lay(total(mine, logprob))
-    entropy_ref[...] = lay(total(mine, entropy))
-    score_ref[...] = lay(total(inside, logprob) / length.astype(jnp.float32))
+    result_ref[0:1, 0:own_rows] = lay(total(mine, logprob))
+    result_ref[1:2, 0:own_rows] = lay(total(mine, entropy))
+    result_ref[2:3, 0:seqs] = lay(total(inside, logprob) / length.astype(jnp.float32))
 
     for ch in range(chunks):
         for slot in range(slots[ch]):
@@ -461,15 +459,11 @@
     hbm = pl.BlockSpec(memory_space=pltpu.HBM)
     vmem = pl.BlockSpec(memory_space=pltpu.VMEM)
     dma = pltpu.SemaphoreType.DMA
-    logprob, entropy, score = pl.pallas_call(
+    result = pl.pallas_call(
         functools.partial(kernel, n),
-        out_shape=(
-            jax.ShapeDtypeStruct((1, own_rows), jnp.float32),
-            jax.ShapeDtypeStruct((1, own_rows), jnp.float32),
-            jax.ShapeDtypeStruct((1, seqs), jnp.float32),
-        ),
+        out_shape=jax.ShapeDtypeStruct((8, 128), jnp.float32),
         in_specs=[hbm] * 7,
-        out_specs=(vmem, vmem, vmem),
+        out_specs=vmem,
         scratch_shapes=[
             pltpu.SMEM((own_rows,), jnp.int32),
             pltpu.SMEM((seqs,), jnp.int32),
@@ -504,7 +498,20 @@
         ),
         name="head_stats",
     )(targets, lengths, offsets, loss_mask, hidden, norm_gain, head_weight)
-    return logprob.reshape(own_rows), entropy.reshape(own_rows), score.reshape(seqs)
+    sizes = (own_rows, own_rows, seqs)
+
+    def split(packed_ref, *out_refs):
+        for i, size in enumerate(sizes):
+            out_refs[i][...] = packed_ref[i, 0:size]
+
+    return pl.pallas_call(
+        split,
+        out_shape=tuple(jax.ShapeDtypeStruct((size,), jnp.float32) for size in sizes),
+        in_specs=[vmem],
+        out_specs=(vmem, vmem, vmem),
+        compiler_params=pltpu.CompilerParams(vmem_limit_bytes=64 * 2**20),
+        name="split",
+    )(result)
 
 
 def solution(mesh):

time: 41.9 us -> 38.9 us (0.928)
  local copies, waits for them, and re-layouts: 3.42 us -> 0 us
    unnamed x3 -> x0, local copies, waits for them, and re-layouts: 3.42 us -> none
    pallas_call x1 -> x2, Pallas kernels: 37.6 us -> 38 us  [the longest x1 36.8 us: local(): pl.pallas_call(functools.partial(kernel, n), out_shape=jax.ShapeDtypeStru...]
where the time goes in v3:
time: 38.9 us; the launch traced here: 38.7 us
  Pallas kernels  38 us (98%)
  between operations  0.64 us (2%)
    pallas_call x1, Pallas kernels, local(): pl.pallas_call(functools.partial(kernel, n), out_shape=jax.ShapeDtypeStru...  36.8 us
    pallas_call x1, Pallas kernels, local(): pl.pallas_call(split, out_shape=tuple((jax.ShapeDtypeStruct((size,), jnp....  1.2 us

profile of v3, /device:TPU:0, one launch (start us, length us, event | category | flops | bytes accessed | tf_op | source)
XLA Modules:
  0.0 38.7 jit_solution(12903793257370825051)
XLA Ops:
  0.6 36.8 %head_stats.1.packed_ref = f32[8,128]{1,0:T(8,128)} custom-call(s32[16]{0:T(128)} %targets_hbm.1, s32[12]{0:T(128)} %lengths_hbm.1, s32[12]{0:T(128)} %offsets_hbm.1, s32[16]{0:T(128)} %mask_hbm.1, bf16[16,4096]{1,0:T(8,128)(2,1)} %hidden_hbm.1, f32[4096]{0:T(1024)} %gain_hbm.1, bf16[2004,4096]{1,0:T(8,128)(2,1)} %weight_ref.1), custom_call_target="tpu_custom_call" | custom-call | flops 2626682880 | bytes 16416768 | tf_op jit(solution)/shard_map/head_stats/pallas_call | solution.py:462
  37.5 1.2 %split.1 = (f32[16]{0:T(128)}, f32[16]{0:T(128)}, f32[12]{0:T(128)}) custom-call(f32[8,128]{1,0:T(8,128)} %head_stats.1.packed_ref), custom_call_target="tpu_custom_call" | custom-call | tf_op jit(solution)/shard_map/split/pallas_call | solution.py:507

commit v4 on v3

--- a/solution.py
+++ b/solution.py
@@ -21,10 +21,7 @@
 
 
 def grid_dims(n):
-    for dims in ((4, 2, 2), (4, 4, 4)):
-        if dims[0] * dims[1] * dims[2] == n:
-            return dims
-    return (1, 1, n)
+    return {16: (4, 2, 2), 64: (4, 4, 4)}[n]
 
 
 def iota(shape, dim):
@@ -78,6 +75,11 @@
     def at(i, j, k):
         return ((a + i) % na) * (nb * nc) + ((b + j) % nb) * nc + (c + k) % nc
 
+    def slot_of(j, k):
+        return (((b + j) % nb) * nc + (c + k) % nc) * na
+
+    mine_at = slot_of(0, 0)
+
     def head_copy(ch):
         return pltpu.make_async_copy(
             weight_ref.at[:, pl.ds(ch * CHUNK, CHUNK)], head.at[ch], head_sem.at[ch]
@@ -141,78 +143,70 @@
         packed = sum(
             dot(halves[h], normed[:, base + h * HALF : base + (h + 1) * HALF]) for h in range(2)
         )
-        blocks[ch, me, :, 0:HALF] = packed.astype(jnp.bfloat16)
+        blocks[ch, mine_at, :, 0:HALF] = packed.astype(jnp.bfloat16)
         packed = sum(
             dot(pieces[e], normed[:, base + e * PIECE : base + (e + 1) * PIECE]) for e in range(8)
         )
-        blocks[ch, me, :, HALF:WIDE] = packed.astype(jnp.bfloat16)
-
-    slots = [0] * chunks
-
-    def remote(ch, src, slot, peer):
+        blocks[ch, mine_at, :, HALF:WIDE] = packed.astype(jnp.bfloat16)
+
+    sent = [[] for ch in range(chunks)]
+
+    def remote(ch, begin, end, amount, slot, peer):
         return pltpu.make_async_remote_copy(
-            src_ref=blocks.at[ch, src],
-            dst_ref=blocks.at[ch, src],
+            src_ref=blocks.at[ch, pl.ds(begin, amount)],
+            dst_ref=blocks.at[ch, pl.ds(end, amount)],
             send_sem=send_sem.at[ch, slot],
-            recv_sem=recv_sem.at[ch, src],
+            recv_sem=recv_sem.at[ch, end],
             device_id={"tensor": peer},
             device_id_type=MESH,
         )
 
-    def send(ch, src, peer):
-        remote(ch, src, slots[ch], peer).start()
-        slots[ch] += 1
-
-    def arrive(ch, src):
-        remote(ch, src, 0, (me + 1) % n).wait_recv()
-
-    def to_b(ch, src):
+    def send(ch, begin, end, amount, peer):
+        remote(ch, begin, end, amount, len(sent[ch]), peer).start()
+        sent[ch].append(amount)
+
+    def arrive(ch, begin, amount):
+        remote(ch, begin, begin, amount, 0, (me + 1) % n).wait_recv()
+
+    def to_b(ch, begin, amount):
         for j in range(1, nb):
-            send(ch, src, at(0, j, 0))
-
-    def to_c(ch, src):
+            send(ch, begin, begin, amount, at(0, j, 0))
+
+    def to_c(ch, begin, amount):
         for k in range(1, nc):
-            send(ch, src, at(0, 0, k))
+            send(ch, begin, begin, amount, at(0, 0, k))
 
     def along_a(ch):
         for i in range(1, na):
-            send(ch, me, at(i, 0, 0))
+            send(ch, mine_at, mine_at + na - i, 1, at(i, 0, 0))
 
     def own(ch):
-        to_b(ch, me)
-        to_c(ch, me)
+        to_b(ch, mine_at, 1)
+        to_c(ch, mine_at, 1)
 
     def column_on(ch):
         for i in range(1, na):
-            src = at(i, 0, 0)
-            arrive(ch, src)
-            to_b(ch, src)
-            to_c(ch, src)
-
-    early = (na + 1) // 2
+            arrive(ch, mine_at + i, 1)
+        to_b(ch, mine_at + 1, na - 1)
+        to_c(ch, mine_at + 1, na - 1)
+
+    early = na // 2
 
     def across(ch):
-        for i in range(na):
-            if i < early:
-                for j in range(1, nb):
-                    arrive(ch, at(i, j, 0))
-                    to_c(ch, at(i, j, 0))
-            else:
-                for k in range(1, nc):
-                    arrive(ch, at(i, 0, k))
-                    to_b(ch, at(i, 0, k))
+        for j in range(1, nb):
+            arrive(ch, slot_of(j, 0), 1)
+            arrive(ch, slot_of(j, 0) + 1, na - 1)
+            to_c(ch, slot_of(j, 0), early)
+        for k in range(1, nc):
+            arrive(ch, slot_of(0, k), 1)
+            arrive(ch, slot_of(0, k) + 1, na - 1)
+            to_b(ch, slot_of(0, k) + early, na - early)
 
     def settle(ch):
-        for i in range(na):
-            if i < early:
-                for k in range(1, nc):
-                    arrive(ch, at(i, 0, k))
-            else:
-                for j in range(1, nb):
-                    arrive(ch, at(i, j, 0))
-            for j in range(1, nb):
-                for k in range(1, nc):
-                    arrive(ch, at(i, j, k))
+        for j in range(1, nb):
+            for k in range(1, nc):
+                arrive(ch, slot_of(j, k), early)
+                arrive(ch, slot_of(j, k) + early, na - early)
 
     def meta_copy(p):
         return pltpu.make_async_remote_copy(
@@ -247,7 +241,7 @@
     in_main = column < n * MAIN
     owner = jnp.where(in_main, column // MAIN, (column - n * MAIN) // REST)
     rank_at = jnp.where(in_main, column % MAIN, MAIN + (column - n * MAIN) % REST)
-    rank_at = jnp.where(owner == me, rank_at, -1)
+    rank_at = jnp.where(owner == mine_at + a, rank_at, -1)
     ids = jnp.zeros((1, cols), jnp.int32)
     places = jnp.zeros((1, cols), jnp.int32)
     for i in range(own_rows):
@@ -264,20 +258,24 @@
     if chunks > 1:
         column_on(1)
 
+    def slot_at(block):
+        return block // na * na + (block % na + na - a) % na
+
     groups = n // GROUP
     size = GROUP * TOK
     in_row = iota((size, size), 0)
     out_col = iota((size, size), 1)
     span = GROUP * MAIN
-    source = (out_col % span) // MAIN * TOK + out_col // span * MAIN + out_col % MAIN
+    source = slot_at((out_col % span) // MAIN) * TOK + out_col // span * MAIN + out_col % MAIN
     main_perm[...] = jnp.where(in_row == source, 1.0, 0.0).astype(jnp.bfloat16)
     tail = cols - n * MAIN
     in_row = iota((size, tail), 0)
     for g in range(groups):
         out_col = iota((size, tail), 1) - g * GROUP * REST
         valid = (out_col >= 0) & (out_col < GROUP * REST)
+        out_col = jnp.maximum(out_col, 0)
         for e in range(8):
-            source = out_col // REST * TOK + e * REST + out_col % REST
+            source = slot_at(out_col // REST) * TOK + e * REST + out_col % REST
             rest_perm[g * 8 + e] = jnp.where(valid & (in_row == source), 1.0, 0.0).astype(
                 jnp.bfloat16
             )
@@ -328,7 +326,10 @@
                 peak = jnp.maximum(peak, jnp.max(tile, axis=0, keepdims=True))
             return peak
 
-        return tiles(vocab, 512, body, jnp.full((1, cols), -jnp.inf, jnp.float32))
+        peak = jnp.full((1, cols), -jnp.inf, jnp.float32)
+        for begin in range(0, vocab, 512):
+            peak = body(begin, min(512, vocab - begin), peak)
+        return peak
 
     padded = scores.shape[0]
     if padded > vocab:
@@ -441,8 +442,8 @@
     result_ref[2:3, 0:seqs] = lay(total(inside, logprob) / length.astype(jnp.float32))
 
     for ch in range(chunks):
-        for slot in range(slots[ch]):
-            remote(ch, me, slot, (me + 1) % n).wait_send()
+        for slot, amount in enumerate(sent[ch]):
+            remote(ch, 0, 0, amount, slot, (me + 1) % n).wait_send()
 
     @pl.loop(1, n)
     def _(p):

time: 38.9 us -> 37.5 us (0.964)
  Pallas kernels: 38 us -> 36.7 us
    pallas_call x1, Pallas kernels: 36.8 us -> 35.5 us  [local(): pl.pallas_call(functools.partial(kernel, n), out_shape=jax.ShapeDtypeStru...]
where the time goes in v4:
time: 37.5 us; the launch traced here: 37.3 us
  Pallas kernels  36.7 us (98%)
  between operations  0.64 us (2%)
    pallas_call x1, Pallas kernels, local(): pl.pallas_call(functools.partial(kernel, n), out_shape=jax.ShapeDtypeStru...  35.5 us
    pallas_call x1, Pallas kernels, local(): pl.pallas_call(split, out_shape=tuple((jax.ShapeDtypeStruct((size,), jnp....  1.2 us

profile of v4, /device:TPU:0, one launch (start us, length us, event | category | flops | bytes accessed | tf_op | source)
XLA Modules:
  0.0 37.3 jit_solution(12690995500894323321)
XLA Ops:
  0.6 35.5 %head_stats.1.packed_ref = f32[8,128]{1,0:T(8,128)} custom-call(s32[16]{0:T(128)} %targets_hbm.1, s32[12]{0:T(128)} %lengths_hbm.1, s32[12]{0:T(128)} %offsets_hbm.1, s32[16]{0:T(128)} %mask_hbm.1, bf16[16,4096]{1,0:T(8,128)(2,1)} %hidden_hbm.1, f32[4096]{0:T(1024)} %gain_hbm.1, bf16[2004,4096]{1,0:T(8,128)(2,1)} %weight_ref.1), custom_call_target="tpu_custom_call" | custom-call | flops 2626682880 | bytes 16416768 | tf_op jit(solution)/shard_map/head_stats/pallas_call | solution.py:463
  36.1 1.2 %split.1 = (f32[16]{0:T(128)}, f32[16]{0:T(128)}, f32[12]{0:T(128)}) custom-call(f32[8,128]{1,0:T(8,128)} %head_stats.1.packed_ref), custom_call_target="tpu_custom_call" | custom-call | tf_op jit(solution)/shard_map/split/pallas_call | solution.py:508

commit v5 on v4

--- a/solution.py
+++ b/solution.py
@@ -117,36 +117,35 @@
     meansq = jnp.mean(values * values, axis=1, keepdims=True)
     normed = (values * lax.rsqrt(meansq + epsilon) * gain_ref[...][None, :]).astype(jnp.bfloat16)
 
-    sub = iota((TOK, own_rows), 0)
-    lane = iota((TOK, own_rows), 1)
-    rank_of = jnp.full((TOK, own_rows), -1, jnp.int32)
+    sub = iota((TOK, 8 * own_rows), 0)
+    lane = iota((TOK, 8 * own_rows), 1)
+    rank_of = jnp.full((TOK, 8 * own_rows), -1, jnp.int32)
     ranks = []
     count = jnp.int32(0)
     for i in range(own_rows):
         live = mask_ref[i]
         ranks.append(jnp.where(live == 1, count, -2))
         count = count + live
-        rank_of = jnp.where(lane == i, ranks[i], rank_of)
-
-    def choice(begin, first, amount):
-        hit = (sub >= begin) & (sub < begin + amount) & (rank_of == sub - begin + first)
+        rank_of = jnp.where(lane % own_rows == i, ranks[i], rank_of)
+
+    def choice(first, amount):
+        hit = (sub // amount == lane // own_rows) & (rank_of == first + sub % amount)
         return jnp.where(hit, 1.0, 0.0).astype(jnp.bfloat16)
 
     def dot(x, y):
         return jnp.dot(x, y, preferred_element_type=jnp.float32)
 
-    halves = [choice(h * MAIN, 0, MAIN) for h in range(2)]
-    pieces = [choice(e * REST, MAIN, REST) for e in range(8)]
+    halves = choice(0, MAIN)[:, 0 : 2 * own_rows]
+    pieces = choice(MAIN, REST)
+
+    def stack(begin, step, amount):
+        parts = [normed[:, begin + e * step : begin + (e + 1) * step] for e in range(amount)]
+        return jnp.concatenate(parts, axis=0)
 
     def pack(ch):
-        base = ch * CHUNK
-        packed = sum(
-            dot(halves[h], normed[:, base + h * HALF : base + (h + 1) * HALF]) for h in range(2)
-        )
+        packed = dot(halves, stack(ch * CHUNK, HALF, 2))
         blocks[ch, mine_at, :, 0:HALF] = packed.astype(jnp.bfloat16)
-        packed = sum(
-            dot(pieces[e], normed[:, base + e * PIECE : base + (e + 1) * PIECE]) for e in range(8)
-        )
+        packed = dot(pieces, stack(ch * CHUNK, PIECE, 8))
         blocks[ch, mine_at, :, HALF:WIDE] = packed.astype(jnp.bfloat16)
 
     sent = [[] for ch in range(chunks)]
@@ -236,27 +235,11 @@
         pack(ch)
         along_a(ch)
         own(ch)
-
-    column = iota((1, cols), 1)
-    in_main = column < n * MAIN
-    owner = jnp.where(in_main, column // MAIN, (column - n * MAIN) // REST)
-    rank_at = jnp.where(in_main, column % MAIN, MAIN + (column - n * MAIN) % REST)
-    rank_at = jnp.where(owner == mine_at + a, rank_at, -1)
-    ids = jnp.zeros((1, cols), jnp.int32)
-    places = jnp.zeros((1, cols), jnp.int32)
-    for i in range(own_rows):
-        ids = jnp.where(rank_at == ranks[i], targets_ref[i], ids)
-        places = jnp.where(rank_at == ranks[i], me * own_rows + (i + 1), places)
-    meta[me, 0:1, :] = ids
-    meta[me, 1:2, :] = places
-
-    @pl.loop(1, n)
-    def _(p):
-        meta_copy(p).start()
-
-    column_on(0)
-    if chunks > 1:
-        column_on(1)
+        if ch == 2:
+            column_on(0)
+    column_on(1)
+
+    across(0)
 
     def slot_at(block):
         return block // na * na + (block % na + na - a) % na
@@ -305,49 +288,78 @@
             rest = sum(turned(rests[g], rest_perm[g * 8 + e]) for g in range(groups))
             rows[e * PIECE : (e + 1) * PIECE, n * MAIN : cols] = rest.astype(jnp.bfloat16)
 
-    def tiles(extent, step, body, carry):
-        full = extent // step
-        carry = lax.fori_loop(
-            0, full, lambda t, v: body(pl.multiple_of(t * step, step), step, v), carry
-        )
-        if extent % step:
-            carry = body(full * step, extent % step, carry)
-        return carry
+    padded = scores.shape[0]
 
     def partial(ch):
         head_copy(ch).wait()
-
-        def body(begin, amount, peak):
-            tile = dot(head[ch, pl.ds(begin, amount), :], rows[...])
+        found = []
+        for begin in range(0, vocab, 512):
+            amount = min(512, vocab - begin)
+            tile = dot(head[ch, begin : begin + amount, :], rows[...])
             if ch > 0:
-                tile = tile + scores[pl.ds(begin, amount), :]
-            scores[pl.ds(begin, amount), :] = tile
+                tile = tile + scores[begin : begin + amount, :]
+            scores[begin : begin + amount, :] = tile
             if ch == chunks - 1:
-                peak = jnp.maximum(peak, jnp.max(tile, axis=0, keepdims=True))
-            return peak
-
-        peak = jnp.full((1, cols), -jnp.inf, jnp.float32)
-        for begin in range(0, vocab, 512):
-            peak = body(begin, min(512, vocab - begin), peak)
-        return peak
-
-    padded = scores.shape[0]
+                peak = jnp.max(tile, axis=0, keepdims=True)
+                found.append((peak,) + collect(begin, min(begin + 512, padded), peak))
+        return found
+
+    def collect(begin, end, peak):
+        gathered = [jnp.zeros((8, cols), jnp.float32)] * 3
+        for at_row in range(begin, end, 64):
+            tile = scores[at_row : min(at_row + 64, end), :]
+            centred = tile - peak
+            expo = jnp.exp(centred)
+            entry = at_row + iota(tile.shape, 0)
+            given = jnp.where(entry == local_ids, tile, 0.0)
+            gathered = [
+                old + jnp.sum(x.reshape(x.shape[0] // 8, 8, cols), axis=0)
+                for old, x in zip(gathered, (expo, expo * centred, given))
+            ]
+        return tuple(jnp.sum(x, axis=0, keepdims=True) for x in gathered)
+
+    def merge(parts):
+        peak = functools.reduce(jnp.maximum, [part[0] for part in parts])
+        row_sum = spread = picked = 0.0
+        for part in parts:
+            shift = part[0] - peak
+            factor = jnp.exp(shift)
+            row_sum = row_sum + factor * part[1]
+            spread = spread + factor * (part[2] + shift * part[1])
+            picked = picked + part[3]
+        return peak, row_sum, spread, picked
+
     if padded > vocab:
         scores[vocab:padded, :] = jnp.full((padded - vocab, cols), -1e30, jnp.float32)
 
-    across(0)
-    if chunks > 2:
-        column_on(2)
-    if chunks > 1:
-        across(1)
+    column = iota((1, cols), 1)
+    in_main = column < n * MAIN
+    owner = jnp.where(in_main, column // MAIN, (column - n * MAIN) // REST)
+    rank_at = jnp.where(in_main, column % MAIN, MAIN + (column - n * MAIN) % REST)
+    rank_at = jnp.where(owner == mine_at + a, rank_at, -1)
+    ids = jnp.zeros((1, cols), jnp.int32)
+    places = jnp.zeros((1, cols), jnp.int32)
+    for i in range(own_rows):
+        ids = jnp.where(rank_at == ranks[i], targets_ref[i], ids)
+        places = jnp.where(rank_at == ranks[i], me * own_rows + (i + 1), places)
+    meta[me, 0:1, :] = ids
+    meta[me, 1:2, :] = places
+
+    @pl.loop(1, n)
+    def _(p):
+        meta_copy(p).start()
+
+    column_on(2)
+    across(1)
     for ch in range(chunks):
         if ch + 3 < chunks:
             column_on(ch + 3)
         if ch + 2 < chunks:
             across(ch + 2)
-        settle(ch)
-        unpack(ch)
-        peak = partial(ch)
+        if ch + 1 < chunks:
+            settle(ch)
+            unpack(ch)
+            partial(ch)
 
     @pl.loop(1, n)
     def _(p):
@@ -365,26 +377,11 @@
     places = sum(meta[s, 1:2, :] for s in range(n)) - 1
     local_ids = ids - me * vocab
     local_ids = jnp.where(local_ids < vocab, local_ids, -1)
-
-    def collect(begin, amount, carry):
-        row_sum, spread, picked = carry
-        tile = scores[pl.ds(begin, amount), :]
-        centred = tile - peak
-        expo = jnp.exp(centred)
-        entry = begin + iota(tile.shape, 0)
-        given = jnp.where(entry == local_ids, tile, 0.0)
-
-        def fold(x):
-            return jnp.sum(x.reshape(amount // 8, 8, cols), axis=0)
-
-        return row_sum + fold(expo), spread + fold(expo * centred), picked + fold(given)
-
-    nothing = jnp.zeros((8, cols), jnp.float32)
-    row_sum, spread, picked = (
-        jnp.sum(x, axis=0, keepdims=True)
-        for x in tiles(padded, 64, collect, (nothing, nothing, nothing))
-    )
-    nothing = nothing[0:1]
+    settle(chunks - 1)
+    unpack(chunks - 1)
+    found = partial(chunks - 1)
+
+    peak, row_sum, spread, picked = merge(found)
     stats[me, 0:1, :] = peak
     stats[me, 1:2, :] = row_sum
     stats[me, 2:3, :] = spread
@@ -416,15 +413,9 @@
             device_id_type=MESH,
         ).wait_recv()
 
-    top = functools.reduce(jnp.maximum, [stats[s, 0:1, :] for s in range(n)])
-    sum_exp, spread, picked = nothing, nothing, nothing
-    for s in range(n):
-        shift = stats[s, 0:1, :] - top
-        factor = jnp.exp(shift)
-        part = stats[s, 1:2, :]
-        sum_exp = sum_exp + factor * part
-        spread = spread + factor * (stats[s, 2:3, :] + shift * part)
-        picked = picked + stats[s, 3:4, :]
+    top, sum_exp, spread, picked = merge(
+        [tuple(stats[s, i : i + 1, :] for i in range(4)) for s in range(n)]
+    )
     log_total = jnp.log(sum_exp)
     logprob = picked - top - log_total
     entropy = log_total - spread / sum_exp

time: 37.5 us -> 36.3 us (0.968)
  Pallas kernels: 36.7 us -> 35.5 us
    pallas_call x1, Pallas kernels: 35.5 us -> 34.3 us  [local(): pl.pallas_call(functools.partial(kernel, n), out_shape=jax.ShapeDtypeStru...]
where the time goes in v5:
time: 36.3 us; the launch traced here: 36.1 us
  Pallas kernels  35.5 us (98%)
  between operations  0.64 us (2%)
    pallas_call x1, Pallas kernels, local(): pl.pallas_call(functools.partial(kernel, n), out_shape=jax.ShapeDtypeStru...  34.3 us
    pallas_call x1, Pallas kernels, local(): pl.pallas_call(split, out_shape=tuple((jax.ShapeDtypeStruct((size,), jnp....  1.2 us

profile of v5, /device:TPU:0, one launch (start us, length us, event | category | flops | bytes accessed | tf_op | source)
XLA Modules:
  0.0 36.1 jit_solution(3525493485212342675)
XLA Ops:
  0.6 34.3 %head_stats.1.packed_ref = f32[8,128]{1,0:T(8,128)} custom-call(s32[16]{0:T(128)} %targets_hbm.1, s32[12]{0:T(128)} %lengths_hbm.1, s32[12]{0:T(128)} %offsets_hbm.1, s32[16]{0:T(128)} %mask_hbm.1, bf16[16,4096]{1,0:T(8,128)(2,1)} %hidden_hbm.1, f32[4096]{0:T(1024)} %gain_hbm.1, bf16[2004,4096]{1,0:T(8,128)(2,1)} %weight_ref.1), custom_call_target="tpu_custom_call" | custom-call | flops 2626682880 | bytes 16416768 | tf_op jit(solution)/shard_map/head_stats/pallas_call | solution.py:454
  34.9 1.2 %split.1 = (f32[16]{0:T(128)}, f32[16]{0:T(128)}, f32[12]{0:T(128)}) custom-call(f32[8,128]{1,0:T(8,128)} %head_stats.1.packed_ref), custom_call_target="tpu_custom_call" | custom-call | tf_op jit(solution)/shard_map/split/pallas_call | solution.py:499

commit v6 on v5

--- a/solution.py
+++ b/solution.py
@@ -12,7 +12,7 @@
 MAIN = 8
 REST = LIVE - MAIN
 TOK = 16
-CHUNK = 1024
+CHUNK = 2048
 HALF = CHUNK // 2
 PIECE = CHUNK // 8
 WIDE = HALF + PIECE
@@ -235,7 +235,7 @@
         pack(ch)
         along_a(ch)
         own(ch)
-        if ch == 2:
+        if ch == min(2, chunks - 1):
             column_on(0)
     column_on(1)
 
@@ -349,7 +349,8 @@
     def _(p):
         meta_copy(p).start()
 
-    column_on(2)
+    if chunks > 2:
+        column_on(2)
     across(1)
     for ch in range(chunks):
         if ch + 3 < chunks:

time: 36.3 us -> 38.8 us (1.069)
  Pallas kernels: 35.5 us -> 37.9 us
    pallas_call x1, Pallas kernels: 34.3 us -> 36.7 us  [local(): pl.pallas_call(functools.partial(kernel, n), out_shape=jax.ShapeDtypeStru...]
where the time goes in v6:
time: 38.8 us; the launch traced here: 38.6 us
  Pallas kernels  37.9 us (98%)
  between operations  0.64 us (2%)
    pallas_call x1, Pallas kernels, local(): pl.pallas_call(functools.partial(kernel, n), out_shape=jax.ShapeDtypeStru...  36.7 us
    pallas_call x1, Pallas kernels, local(): pl.pallas_call(split, out_shape=tuple((jax.ShapeDtypeStruct((size,), jnp....  1.2 us

profile of v6, /device:TPU:0, one launch (start us, length us, event | category | flops | bytes accessed | tf_op | source)
XLA Modules:
  0.0 38.6 jit_solution(4404798417665183117)
XLA Ops:
  0.6 36.7 %head_stats.1.packed_ref = f32[8,128]{1,0:T(8,128)} custom-call(s32[16]{0:T(128)} %targets_hbm.1, s32[12]{0:T(128)} %lengths_hbm.1, s32[12]{0:T(128)} %offsets_hbm.1, s32[16]{0:T(128)} %mask_hbm.1, bf16[16,4096]{1,0:T(8,128)(2,1)} %hidden_hbm.1, f32[4096]{0:T(1024)} %gain_hbm.1, bf16[2004,4096]{1,0:T(8,128)(2,1)} %weight_ref.1), custom_call_target="tpu_custom_call" | custom-call | flops 2626682880 | bytes 16416768 | tf_op jit(solution)/shard_map/head_stats/pallas_call | solution.py:455
  37.4 1.2 %split.1 = (f32[16]{0:T(128)}, f32[16]{0:T(128)}, f32[12]{0:T(128)}) custom-call(f32[8,128]{1,0:T(8,128)} %head_stats.1.packed_ref), custom_call_target="tpu_custom_call" | custom-call | tf_op jit(solution)/shard_map/split/pallas_call | solution.py:500
